TPU v7x, 512 devices: a whole 4x8x8 slice. The times are simulated.
512 devices in a mesh: head: 8 (over y), blk: 64 (over z, x, core).
Axes of the slice: x: 4, y: 8, z: 8, core: 2. Of those that a mesh axis runs over, the one named last changes fastest.
Arguments:
- residual: bfloat16 [12288, 2048], P('blk'), may hold values from -100 to 100
- lengths: int32 [64, 6], P('blk'), may hold values from 1 to 96, 192 in all within a row
- token_adapter_index: int32 [12288, 1], P('blk'), may hold values from 0 to 63; in each aligned block of 192 rows (0 to 191, 192 to 383, ...) at most 6 rows name the same one
- attention_norm_gain: float32 [2048], replicated, may hold values from 0.1 to 1.9
- query_key_weight: bfloat16 [2048, 4096], P('blk', 'head'), may hold values from -8 to 8
- value_weight: bfloat16 [2048, 2048], P('blk', 'head'), may hold values from -0.125 to 0.125
- head_second_weight: float32 [8], P('head'), may hold values from 0.2 to 0.8
- output_weight: bfloat16 [2048, 2048], P('blk', 'head'), may hold values from -0.125 to 0.125
- adapter_down_maps: bfloat16 [64, 2048, 16], P('blk', 'head'), may hold values from -0.125 to 0.125
- adapter_up_maps: bfloat16 [64, 16, 2048], P('blk'), may hold values from -1.5 to 1.5
- feedforward_norm_gain: float32 [2048], replicated, may hold values from 0.1 to 1.9
- gate_weight: bfloat16 [2048, 5632], P('blk', 'head'), may hold values from -0.125 to 0.125
- up_weight: bfloat16 [2048, 5632], P('blk', 'head'), may hold values from -0.125 to 0.125
- down_weight: bfloat16 [2048, 5632], P('blk', 'head'), may hold values from -0.078125 to 0.078125
Outputs:
- layer_out: bfloat16 [12288, 2048], P('blk', 'head')
Inputs may be any that keep to these rules, and one draw needn't show every extreme that they name: `lengths`: each row sums to 192, and its largest entry is 96. `token_adapter_index`: among the 192 tokens of one block no adapter is named more than 6 times, a bound that some block reaches.
All inputs are finite; a program needn't handle non-finite values.
Results may differ from a plain program's by a relative error of at most 0.011.
Values may be sent and summed in bfloat16 or wider, within the bound.
No kernel may reach another device: no remote copies, remote signals or barrier semaphores. Data moves between devices by JAX's collectives and lax.ppermute only.
A program may use at most 64 MiB of HBM per device.

v0:
```python
import jax
import jax.numpy as jnp
from jax import lax
from jax.sharding import PartitionSpec as P

HD = 128
adapter_scaling = 2.0
head_shrink = 0.8
neg_large = -1e30


def rms_scale(values, epsilon):
    return values * lax.rsqrt(jnp.mean(values * values, axis=-1, keepdims=True) + epsilon)


def masked_softmax(scores, allowed):
    scores = jnp.where(allowed, scores, neg_large)
    row_peak = jnp.max(scores, axis=-1, keepdims=True)
    raised = jnp.where(allowed, jnp.exp(scores - row_peak), 0.0)
    return raised / jnp.sum(raised, axis=-1, keepdims=True)


def request_mask(lengths_row, length_total):
    ends_at = jnp.cumsum(lengths_row)
    position = jnp.arange(length_total, dtype=jnp.int32)
    request = jnp.sum((position[:, None] >= ends_at[None, :]).astype(jnp.int32), axis=1)
    return (request[:, None] == request[None, :]) & (position[None, :] <= position[:, None])


def diff_head(qk_head, value_head, allowed, lambda_value):
    score_scale = 1.0 / qk_head.shape[-1] ** 0.5
    first_scores = (
        jnp.dot(qk_head[:, 0], qk_head[:, 2].T, precision=lax.Precision.HIGHEST) * score_scale
    )
    second_scores = (
        jnp.dot(qk_head[:, 1], qk_head[:, 3].T, precision=lax.Precision.HIGHEST) * score_scale
    )
    mixed = (
        masked_softmax(first_scores, allowed)
        - lambda_value * masked_softmax(second_scores, allowed)
    ).astype(jnp.bfloat16)
    attended = jnp.dot(mixed, value_head, preferred_element_type=jnp.float32)
    return (rms_scale(attended, 1e-05) * head_shrink).astype(jnp.bfloat16)


def weight_fold(leading, trailing, combine, initial):
    return combine(
        initial,
        (
            lax.all_gather(leading, "blk", axis=0, tiled=True),
            lax.all_gather(trailing, "blk", axis=0, tiled=True),
        ),
        jnp.int32(0),
    )


def head_total(partial_value):
    return lax.psum_scatter(
        partial_value.astype(jnp.bfloat16), "head", scatter_dimension=1, tiled=True
    ).astype(jnp.float32)


def row_products(source):

    def add_rows(totals, pieces, offset):
        return (
            jnp.dot(source, pieces[0], preferred_element_type=jnp.float32),
            jnp.dot(source, pieces[1], preferred_element_type=jnp.float32),
        )

    return add_rows


def per_device(
    residual,
    lengths,
    token_adapter_index,
    attention_norm_gain,
    query_key_weight,
    value_weight,
    head_second_weight,
    output_weight,
    adapter_down_maps,
    adapter_up_maps,
    feedforward_norm_gain,
    gate_weight,
    up_weight,
    down_weight,
):
    tokens = residual.shape[0]
    width = residual.shape[1]
    owners = lax.axis_size("blk")
    capacity = 2 * tokens // owners
    own_width = width // lax.axis_size("head")
    own_begin = lax.axis_index("head") * own_width
    inputs = residual.astype(jnp.float32)
    normed = (rms_scale(inputs, 1e-06) * attention_norm_gain).astype(jnp.bfloat16)
    qk_start = jnp.zeros((tokens, query_key_weight.shape[1]), jnp.float32)
    value_start = jnp.zeros((tokens, value_weight.shape[1]), jnp.float32)
    qk_local, value_local = weight_fold(
        query_key_weight, value_weight, row_products(normed), (qk_start, value_start)
    )
    qk_head = qk_local.reshape(tokens, 4, HD)
    value_head = value_local.astype(jnp.bfloat16)
    allowed = request_mask(lengths[0], tokens)
    head_out = diff_head(qk_head, value_head, allowed, head_second_weight[0])
    chosen = token_adapter_index[:, 0]
    owner_ids = jnp.arange(owners, dtype=jnp.int32)
    member = (chosen[:, None] == owner_ids[None, :]).astype(jnp.int32)
    earlier = jnp.cumsum(member, axis=0) - member
    within = jnp.sum(earlier * member, axis=1)
    target = chosen * capacity + within
    slot_ids = jnp.arange(owners * capacity, dtype=jnp.int32)
    dispatch = (slot_ids[:, None] == target[None, :]).astype(jnp.bfloat16)
    outgoing = jnp.dot(dispatch, head_out, preferred_element_type=jnp.float32).astype(jnp.bfloat16)
    outgoing = outgoing.reshape(owners, capacity, head_out.shape[1])
    received = lax.all_to_all(outgoing, "blk", split_axis=0, concat_axis=0, tiled=True)
    sources = received.shape[0]
    slot_count = received.shape[1]
    flat_heads_output = received.reshape(sources * slot_count, received.shape[2])
    reduced_rank_part = jnp.dot(
        flat_heads_output, adapter_down_maps[0], preferred_element_type=jnp.float32
    )
    reduced_rank_state = lax.psum(reduced_rank_part, "head").astype(jnp.bfloat16)
    adapter_delta = (
        adapter_scaling
        * jnp.dot(reduced_rank_state, adapter_up_maps[0], preferred_element_type=jnp.float32)
    ).astype(jnp.bfloat16)
    returned = lax.all_to_all(
        adapter_delta.reshape(sources, slot_count, width),
        "blk",
        split_axis=0,
        concat_axis=0,
        tiled=True,
    )
    delta_rows = lax.dot_general(
        dispatch,
        returned.reshape(owners * capacity, returned.shape[2]),
        (((0,), (0,)), ((), ())),
        preferred_element_type=jnp.float32,
    )
    delta_own = lax.dynamic_slice_in_dim(delta_rows, own_begin, own_width, 1)
    unit_count = down_weight.shape[1]

    def place_columns(totals, pieces, offset):
        columns = lax.dot_general(
            head_out, pieces[0], (((1,), (1,)), ((), ())), preferred_element_type=jnp.float32
        )
        return (columns, pieces[1])

    projected_start = jnp.zeros((tokens, width), jnp.float32)
    down_start = jnp.zeros((width, unit_count), jnp.bfloat16)
    projected, down_full = weight_fold(
        output_weight, down_weight, place_columns, (projected_start, down_start)
    )
    own_mid = (
        lax.dynamic_slice_in_dim(inputs, own_begin, own_width, 1)
        + head_total(projected)
        + delta_own
    )
    mid_full = lax.all_gather(own_mid.astype(jnp.bfloat16), "head", axis=1, tiled=True)
    ffn_in = (rms_scale(mid_full.astype(jnp.float32), 1e-06) * feedforward_norm_gain).astype(
        jnp.bfloat16
    )
    gate_start = jnp.zeros((tokens, gate_weight.shape[1]), jnp.float32)
    up_start = jnp.zeros((tokens, up_weight.shape[1]), jnp.float32)
    gate_act, upward = weight_fold(
        gate_weight, up_weight, row_products(ffn_in), (gate_start, up_start)
    )
    hidden_units = (jax.nn.silu(gate_act) * upward).astype(jnp.bfloat16)
    ffn_part = lax.dot_general(
        hidden_units, down_full, (((1,), (1,)), ((), ())), preferred_element_type=jnp.float32
    )
    return (own_mid + head_total(ffn_part)).astype(jnp.bfloat16)


def solution(mesh):
    return jax.shard_map(
        per_device,
        mesh=mesh,
        in_specs=(
            P("blk", None),
            P("blk", None),
            P("blk", None),
            P(),
            P("blk", "head"),
            P("blk", "head"),
            P("head"),
            P("blk", "head"),
            P("blk", "head", None),
            P("blk", None, None),
            P(),
            P("blk", "head"),
            P("blk", "head"),
            P("blk", "head"),
        ),
        out_specs=P("blk", "head"),
        check_vma=False,
    )
```

profile of v0, /device:TPU:2, one launch (start us, length us, event | category | flops | bytes accessed | tf_op | source)
XLA Modules:
  0.0 619.7 jit_solution(7784527970061427897)
XLA Ops:
  6.5 0.7 all-gather.7.cloned.1.call-update
  7.3 0.7 all-gather.9.cloned.1.call-update
  8.1 0.7 all-gather.11.cloned.1.call-update
  8.7 0.0 reduce-scatter.3.cloned.1.call-start
  8.8 0.8 reduce-window.18
  9.6 0.1 convert_reduce_fusion
  10.4 1.4 multiply_reduce_fusion
  11.7 86.2 %all-gather.7.cloned.1.call-done = bf16[2048,512]{1,0:T(8,128)(2,1)} async-done(((bf16[32,512]{1,0:T(8,128)(2,1)}), bf16[2048,512]{1,0:T(8,128)(2,1)}) %all-gather.7.cloned.1.call-update) | async-done | bytes 2097168 | tf_op jit(solution)/shard_map/all_gather | solution.py:50
  97.9 2.5 fusion.14
  100.4 0.1 reshape.92
  100.6 0.3 fusion.40
  100.8 0.4 fusion.42
  101.2 0.4 fusion.41
  101.6 0.1 fusion.22
  101.7 79.3 %all-gather.9.cloned.1.call-done = bf16[2048,256]{1,0:T(8,128)(2,1)} async-done(((bf16[32,256]{1,0:T(8,128)(2,1)}), bf16[2048,256]{1,0:T(8,128)(2,1)}) %all-gather.9.cloned.1.call-update) | async-done | bytes 1048592 | tf_op jit(solution)/shard_map/all_gather | solution.py:51
  181.0 2.0 multiply_reduce_fusion.1
  183.0 81.1 %all-gather.11.cloned.1.call-done = bf16[2048,256]{1,0:T(8,128)(2,1)} async-done(((bf16[32,256]{1,0:T(8,128)(2,1)}), bf16[2048,256]{1,0:T(8,128)(2,1)}) %all-gather.11.cloned.1.call-update) | async-done | bytes 1048592 | tf_op jit(solution)/shard_map/all_gather | solution.py:50
  264.1 2.7 convolution_convert_fusion.1
  266.8 0.0 all-gather.13.cloned.1.call-start
  266.9 0.5 all-gather.13.cloned.1.call-update
  267.4 0.5 all-gather.15.cloned.1.call-update
  268.0 0.7 all-gather.17.cloned.1.call-update
  268.8 0.6 reduce-window.19
  269.4 0.2 slice_reduce_fusion
  269.6 0.1 bitcast_bitcast_fusion
  269.8 0.3 convolution_convert_fusion.2
  270.0 0.1 reshape.95
  270.1 19.7 %all_to_all.10 = bf16[64,6,256]{2,1,0:T(8,128)(2,1)S(1)} all-to-all(bf16[64,6,256]{2,1,0:T(8,128)(2,1)S(1)} %reshape.95), channel_id=1, replica_groups=mesh['head'=8,'blk'=64] {'blk'}, dimensions={0} | all-to-all | bytes 393216 | tf_op jit(solution)/shard_map/all_to_all | solution.py:117
  289.8 0.1 reshape.96
  289.9 0.2 fusion.35
  290.1 29.8 %psum.7 = bf16[384,16]{0,1:T(8,128)(2,1)S(1)} all-reduce(f32[384,16]{0,1:T(8,128)S(1)} %fusion.35), channel_id=1, replica_groups=mesh['head'=8,'blk'=64] {'head'}, use_global_device_ids=true, to_apply=%region_12.13 | all-reduce | flops 6144 | bytes 36864 | tf_op jit(solution)/shard_map/psum | solution.py:124
  319.9 0.6 multiply_convert_fusion
  320.4 1.6 reshape.97
  322.0 5.6 all-to-all-start.1
  327.7 0.0 reduce-scatter.5.cloned.1.call-start
  327.7 1.4 convert_element_type.59
  329.1 54.3 %all-to-all-done.1 = bf16[64,6,2048]{2,1,0:T(8,128)(2,1)S(1)} async-done(((bf16[64,6,2048]{2,1,0:T(8,128)(2,1)}), bf16[64,6,2048]{2,1,0:T(8,128)(2,1)S(1)}, u32[]{:S(2)}, u32[]{:S(2)}) %all-to-all-start.1) | async-done | bytes 1572896 | tf_op jit(solution)/shard_map/all_to_all | solution.py:129
  383.4 1.4 reshape.98
  384.8 2.0 fusion.12
  386.9 1.0 fusion.37
  388.0 26.0 %all_gather.24 = bf16[192,2048]{1,0:T(8,128)(2,1)S(1)} all-gather(bf16[192,256]{1,0:T(8,128)(2,1)S(1)} %fusion.37), channel_id=1, replica_groups=mesh['head'=8,'blk'=64] {'head'}, dimensions={1}, use_global_device_ids=true | all-gather | bytes 884736 | tf_op jit(solution)/shard_map/all_gather | solution.py:161
  413.9 0.2 fusion
  414.2 2.7 fusion.17
  417.0 64.8 %all-gather.15.cloned.1.call-done = bf16[2048,704]{1,0:T(8,128)(2,1)} async-done(((bf16[32,704]{1,0:T(8,128)(2,1)}), bf16[2048,704]{1,0:T(8,128)(2,1)}) %all-gather.15.cloned.1.call-update) | async-done | bytes 2883600 | tf_op jit(solution)/shard_map/all_gather | solution.py:51
  481.7 85.3 %all-gather.17.cloned.1.call-done = bf16[2048,704]{1,0:T(8,128)(2,1)} async-done(((bf16[32,704]{1,0:T(8,128)(2,1)}), bf16[2048,704]{1,0:T(8,128)(2,1)}) %all-gather.17.cloned.1.call-update) | async-done | bytes 2883600 | tf_op jit(solution)/shard_map/all_gather | solution.py:51
  567.0 5.7 convolution_convert_fusion
  572.8 38.4 %reduce-scatter.5.cloned.1.call-done = bf16[192,256]{1,0:T(8,128)(2,1)} async-done(((bf16[192,2048]{1,0:T(8,128)(2,1)}), bf16[192,256]{1,0:T(8,128)(2,1)}) %reduce-scatter.5.cloned.1.call-update) | async-done | bytes 98320 | tf_op jit(solution)/shard_map/reduce_scatter | solution.py:58
  611.2 1.7 add_convert_fusion
  (32 shorter events, 0.4 us)
Async XLA Ops:
  6.5 313.3 %copy-start = (bf16[1,16,2048]{2,1,0:T(8,128)(2,1)S(1)}, bf16[1,16,2048]{2,1,0:T(8,128)(2,1)}, u32[]{:S(2)}) copy-start(bf16[1,16,2048]{2,1,0:T(8,128)(2,1)} %param.23) | copy-start | bytes 196612
  6.5 91.4 %all-gather.7.cloned.1.call-start = ((), (), s32[]{:S(2)}) async-start(), calls=%async_computation.4 | async-start | bytes 2129920 | tf_op jit(solution)/shard_map/all_gather | solution.py:50
  7.3 173.7 %all-gather.9.cloned.1.call-start = ((), (), s32[]{:S(2)}) async-start(), calls=%async_computation.5 | async-start | bytes 1064960 | tf_op jit(solution)/shard_map/all_gather | solution.py:51
  8.0 256.1 %all-gather.11.cloned.1.call-start = ((), (), s32[]{:S(2)}) async-start(), calls=%async_computation.6 | async-start | bytes 1064960 | tf_op jit(solution)/shard_map/all_gather | solution.py:50
  8.7 378.2 %reduce-scatter.3.cloned.1.call-start = ((), (), s32[]{:S(2)}) async-start(), calls=%async_computation.7 | async-start | bytes 884736 | tf_op jit(solution)/shard_map/reduce_scatter | solution.py:58
  100.4 80.6 %copy-start.1 = (bf16[192,2048]{1,0:T(8,128)(2,1)S(1)}, bf16[192,2048]{1,0:T(8,128)(2,1)}, u32[]{:S(2)}) copy-start(bf16[192,2048]{1,0:T(8,128)(2,1)} %param.14) | copy-start | bytes 2359300
  100.4 80.6 %copy-start.5 = (f32[2048]{0:T(1024)S(1)}, f32[2048]{0:T(1024)}, u32[]{:S(2)}) copy-start(f32[2048]{0:T(1024)} %param.17) | copy-start | bytes 24580
  182.9 85.8 %copy-start.3 = (s32[192,1]{0,1:T(1,128)S(1)}, s32[192,1]{0,1:T(1,128)}, u32[]{:S(2)}) copy-start(s32[192,1]{0,1:T(1,128)} %param.16) | copy-start | bytes 2308
  266.8 23.1 %copy-start.4 = (bf16[1,256,16]{1,2,0:T(8,128)(2,1)S(1)}, bf16[1,256,16]{1,2,0:T(8,128)(2,1)}, u32[]{:S(2)}) copy-start(bf16[1,256,16]{1,2,0:T(8,128)(2,1)} %param.22) | copy-start | bytes 24580
  266.8 147.4 %all-gather.13.cloned.1.call-start = ((), (), s32[]{:S(2)}) async-start(), calls=%async_computation.8 | async-start | bytes 3194880 | tf_op jit(solution)/shard_map/all_gather | solution.py:50
  267.4 214.3 %all-gather.15.cloned.1.call-start = ((), (), s32[]{:S(2)}) async-start(), calls=%async_computation.9 | async-start | bytes 3194880 | tf_op jit(solution)/shard_map/all_gather | solution.py:51
  268.0 299.0 %all-gather.17.cloned.1.call-start = ((), (), s32[]{:S(2)}) async-start(), calls=%async_computation.10 | async-start | bytes 3194880 | tf_op jit(solution)/shard_map/all_gather | solution.py:51
  322.0 61.4 %all-to-all-start.1 = ((bf16[64,6,2048]{2,1,0:T(8,128)(2,1)}), bf16[64,6,2048]{2,1,0:T(8,128)(2,1)S(1)}, u32[]{:S(2)}, u32[]{:S(2)}) async-start(bf16[64,6,2048]{2,1,0:T(8,128)(2,1)} %reshape.97), calls=%async_computation.2 | async-start | bytes 4194304 | tf_op jit(solution)/shard_map/all_to_all | solution.py:129
  327.7 283.5 %reduce-scatter.5.cloned.1.call-start = ((), (), s32[]{:S(2)}) async-start(), calls=%async_computation.11 | async-start | bytes 884736 | tf_op jit(solution)/shard_map/reduce_scatter | solution.py:58
  386.9 27.3 %copy-start.6 = (f32[2048]{0:T(1024)S(1)}, f32[2048]{0:T(1024)}, u32[]{:S(2)}) copy-start(f32[2048]{0:T(1024)} %param.24) | copy-start | bytes 24580
  416.9 194.2 %copy-start.2 = (bf16[192,256]{1,0:T(8,128)(2,1)S(1)}, bf16[192,256]{1,0:T(8,128)(2,1)}, u32[]{:S(2)}) copy-start(bf16[192,256]{1,0:T(8,128)(2,1)} %reduce-scatter.3.cloned.1.call-done) | copy-start | bytes 294916
Sparse Core Ops, SparseCore 0:
  10.7 87.1 all-gather.6
  101.3 79.6 all-gather.8
  184.3 79.7 all-gather.10
  266.9 38.3 reduce-scatter.2
  309.0 88.1 all-gather.12
  400.9 80.8 all-gather.14
  485.6 81.3 all-gather.16
  572.9 38.2 reduce-scatter.4
where the time goes:
time: 620 us
  waiting for transfers between devices  493 us (80%)
  blocking collectives  75.5 us (12%)
  matrix products  19.4 us (3%)
  between operations  14.3 us (2%)
  other arithmetic  7.53 us (1%)
    all_gather x3, waiting for transfers between devices, weight_fold(): lax.all_gather(trailing, 'blk', axis=0, tiled=True)  229 us
    all_gather x3, waiting for transfers between devices, weight_fold(): lax.all_gather(leading, 'blk', axis=0, tiled=True)  167 us
    all_to_all x1, waiting for transfers between devices, per_device(): lax.all_to_all(adapter_delta.reshape(sources, slot_count, width), 'blk',...  54.3 us
    reduce_scatter x2, waiting for transfers between devices, head_total(): lax.psum_scatter(partial_value.astype(jnp.bfloat16), 'head', scatter_dime...  38.4 us
    psum x1, blocking collectives, per_device(): lax.psum(reduced_rank_part, 'head').astype(jnp.bfloat16)  29.8 us
    all_gather x1, blocking collectives, per_device(): lax.all_gather(own_mid.astype(jnp.bfloat16), 'head', axis=1, tiled=True)  26 us
    all_to_all x1, blocking collectives, per_device(): lax.all_to_all(outgoing, 'blk', split_axis=0, concat_axis=0, tiled=True)  19.7 us
  transfers between devices with their start and end apart: 9, of which 7 were waited for; matrix products, arithmetic and copies ran while one was open for 3% of the time, Pallas kernels for 0%

commit v1 on v0

--- a/solution.py
+++ b/solution.py
@@ -121,7 +121,9 @@
     reduced_rank_part = jnp.dot(
         flat_heads_output, adapter_down_maps[0], preferred_element_type=jnp.float32
     )
-    reduced_rank_state = lax.psum(reduced_rank_part, "head").astype(jnp.bfloat16)
+    reduced_rank_state = jnp.sum(lax.all_gather(reduced_rank_part, "head"), axis=0).astype(
+        jnp.bfloat16
+    )
     adapter_delta = (
         adapter_scaling
         * jnp.dot(reduced_rank_state, adapter_up_maps[0], preferred_element_type=jnp.float32)

time: 620 us -> 620 us (level)
  blocking collectives: 75.5 us -> 52.1 us
  waiting for transfers between devices: 493 us -> 508 us
  starting transfers between devices: 5.91 us -> 13.5 us
    psum x1 -> x0, blocking collectives: 29.8 us -> none  [per_device(): lax.psum(reduced_rank_part, 'head').astype(jnp.bfloat16)]
    all_gather x0 -> x1, blocking collectives: none -> 26 us  [per_device(): lax.all_gather(reduced_rank_part, 'head')]
    all_to_all x1 -> x0, blocking collectives: 19.7 us -> none  [per_device(): lax.all_to_all(outgoing, 'blk', split_axis=0, concat_axis=0, tiled=True)]
    all_to_all x0 -> x1, waiting for transfers between devices: none -> 11.5 us  [per_device(): lax.all_to_all(outgoing, 'blk', split_axis=0, concat_axis=0, tiled=True)]
    all_to_all x0 -> x1, starting transfers between devices: none -> 7.68 us  [per_device(): lax.all_to_all(outgoing, 'blk', split_axis=0, concat_axis=0, tiled=True)]
  transfers between devices with their start and end apart: 9 -> 10, of which waited for: 7 -> 8; matrix products, arithmetic and copies ran while one was open for 3% -> 3% of each run, Pallas kernels for 0% -> 0%
where the time goes in v1:
time: 620 us; the launch traced here: 619 us
  waiting for transfers between devices  508 us (82%)
  blocking collectives  52.1 us (8%)
  matrix products  19.4 us (3%)
  between operations  14.4 us (2%)
  starting transfers between devices  13.5 us (2%)
  other arithmetic  7.59 us (1%)
    all_gather x3, waiting for transfers between devices, weight_fold(): lax.all_gather(trailing, 'blk', axis=0, tiled=True)  234 us
    all_gather x3, waiting for transfers between devices, weight_fold(): lax.all_gather(leading, 'blk', axis=0, tiled=True)  167 us
    all_to_all x1, waiting for transfers between devices, per_device(): lax.all_to_all(adapter_delta.reshape(sources, slot_count, width), 'blk',...  53 us
    reduce_scatter x2, waiting for transfers between devices, head_total(): lax.psum_scatter(partial_value.astype(jnp.bfloat16), 'head', scatter_dime...  38.4 us
    all_gather x1, blocking collectives, per_device(): lax.all_gather(own_mid.astype(jnp.bfloat16), 'head', axis=1, tiled=True)  26.1 us
    all_gather x1, blocking collectives, per_device(): lax.all_gather(reduced_rank_part, 'head')  26 us
  transfers between devices with their start and end apart: 10, of which 8 were waited for; matrix products, arithmetic and copies ran while one was open for 3% of the time, Pallas kernels for 0%

profile of v1, /device:TPU:2, one launch (start us, length us, event | category | flops | bytes accessed | tf_op | source)
XLA Modules:
  0.0 619.5 jit_solution(2653456534404462558)
XLA Ops:
  6.5 0.7 all-gather.8.cloned.1.call-update
  7.3 0.7 all-gather.10.cloned.1.call-update
  8.1 0.7 all-gather.12.cloned.1.call-update
  8.8 0.8 reduce-window.18
  9.6 0.1 convert_reduce_fusion
  10.4 1.4 multiply_reduce_fusion
  11.7 86.2 %all-gather.8.cloned.1.call-done = bf16[2048,512]{1,0:T(8,128)(2,1)} async-done(((bf16[32,512]{1,0:T(8,128)(2,1)}), bf16[2048,512]{1,0:T(8,128)(2,1)}) %all-gather.8.cloned.1.call-update) | async-done | bytes 2097168 | tf_op jit(solution)/shard_map/all_gather | solution.py:50
  97.9 2.5 fusion.14
  100.4 0.1 reshape.92
  100.6 0.3 fusion.40
  100.8 0.4 fusion.42
  101.2 0.4 fusion.41
  101.6 0.1 fusion.22
  101.7 79.3 %all-gather.10.cloned.1.call-done = bf16[2048,256]{1,0:T(8,128)(2,1)} async-done(((bf16[32,256]{1,0:T(8,128)(2,1)}), bf16[2048,256]{1,0:T(8,128)(2,1)}) %all-gather.10.cloned.1.call-update) | async-done | bytes 1048592 | tf_op jit(solution)/shard_map/all_gather | solution.py:51
  181.0 2.0 multiply_reduce_fusion.1
  183.0 81.1 %all-gather.12.cloned.1.call-done = bf16[2048,256]{1,0:T(8,128)(2,1)} async-done(((bf16[32,256]{1,0:T(8,128)(2,1)}), bf16[2048,256]{1,0:T(8,128)(2,1)}) %all-gather.12.cloned.1.call-update) | async-done | bytes 1048592 | tf_op jit(solution)/shard_map/all_gather | solution.py:50
  264.1 2.7 convolution_convert_fusion.1
  266.9 0.5 all-gather.14.cloned.1.call-update
  267.4 0.5 all-gather.16.cloned.1.call-update
  268.0 0.6 reduce-window.19
  268.6 0.2 slice_reduce_fusion
  268.9 0.1 bitcast_bitcast_fusion
  269.0 0.3 convolution_convert_fusion.2
  269.3 0.8 reshape.95
  270.1 7.7 %all-to-all-start = ((bf16[64,6,256]{2,1,0:T(8,128)(2,1)}), bf16[64,6,256]{2,1,0:T(8,128)(2,1)S(1)}, u32[]{:S(2)}, u32[]{:S(2)}) async-start(bf16[64,6,256]{2,1,0:T(8,128)(2,1)} %reshape.95), calls=%async_computation.1 | async-start | bytes 524288 | tf_op jit(solution)/shard_map/all_to_all | solution.py:117
  277.8 0.7 all-gather.18.cloned.1.call-update
  278.5 11.5 %all-to-all-done = bf16[64,6,256]{2,1,0:T(8,128)(2,1)S(1)} async-done(((bf16[64,6,256]{2,1,0:T(8,128)(2,1)}), bf16[64,6,256]{2,1,0:T(8,128)(2,1)S(1)}, u32[]{:S(2)}, u32[]{:S(2)}) %all-to-all-start) | async-done | bytes 196640 | tf_op jit(solution)/shard_map/all_to_all | solution.py:117
  290.0 0.1 reshape.96
  290.1 0.2 fusion.35
  290.2 26.0 %all-gather = f32[3072,16]{0,1:T(8,128)S(1)} all-gather(f32[384,16]{0,1:T(8,128)S(1)} %fusion.35), channel_id=2, replica_groups=mesh['head'=8,'blk'=64] {'head'}, dimensions={0}, use_global_device_ids=true | all-gather | bytes 221184 | tf_op jit(solution)/shard_map/all_gather | solution.py:124
  316.2 0.1 bitcast_reduce_fusion
  316.3 0.6 multiply_convert_fusion
  316.9 1.6 reshape.97
  318.5 5.6 all-to-all-start.1
  324.1 0.0 reduce-scatter.5.cloned.1.call-start
  324.1 1.4 convert_element_type.59
  325.5 53.0 %all-to-all-done.1 = bf16[64,6,2048]{2,1,0:T(8,128)(2,1)S(1)} async-done(((bf16[64,6,2048]{2,1,0:T(8,128)(2,1)}), bf16[64,6,2048]{2,1,0:T(8,128)(2,1)S(1)}, u32[]{:S(2)}, u32[]{:S(2)}) %all-to-all-start.1) | async-done | bytes 1572896 | tf_op jit(solution)/shard_map/all_to_all | solution.py:131
  378.5 1.4 reshape.98
  379.9 2.1 fusion.12
  382.0 1.0 fusion.37
  383.1 26.1 %all_gather.32 = bf16[192,2048]{1,0:T(8,128)(2,1)S(1)} all-gather(bf16[192,256]{1,0:T(8,128)(2,1)S(1)} %fusion.37), channel_id=1, replica_groups=mesh['head'=8,'blk'=64] {'head'}, dimensions={1}, use_global_device_ids=true | all-gather | bytes 884736 | tf_op jit(solution)/shard_map/all_gather | solution.py:163
  409.2 0.2 fusion
  409.4 2.7 fusion.17
  412.2 69.4 %all-gather.16.cloned.1.call-done = bf16[2048,704]{1,0:T(8,128)(2,1)} async-done(((bf16[32,704]{1,0:T(8,128)(2,1)}), bf16[2048,704]{1,0:T(8,128)(2,1)}) %all-gather.16.cloned.1.call-update) | async-done | bytes 2883600 | tf_op jit(solution)/shard_map/all_gather | solution.py:51
  481.6 85.3 %all-gather.18.cloned.1.call-done = bf16[2048,704]{1,0:T(8,128)(2,1)} async-done(((bf16[32,704]{1,0:T(8,128)(2,1)}), bf16[2048,704]{1,0:T(8,128)(2,1)}) %all-gather.18.cloned.1.call-update) | async-done | bytes 2883600 | tf_op jit(solution)/shard_map/all_gather | solution.py:51
  566.8 5.7 convolution_convert_fusion
  572.6 38.4 %reduce-scatter.5.cloned.1.call-done = bf16[192,256]{1,0:T(8,128)(2,1)} async-done(((bf16[192,2048]{1,0:T(8,128)(2,1)}), bf16[192,256]{1,0:T(8,128)(2,1)}) %reduce-scatter.5.cloned.1.call-update) | async-done | bytes 98320 | tf_op jit(solution)/shard_map/reduce_scatter | solution.py:58
  611.0 1.7 add_convert_fusion
  (35 shorter events, 0.5 us)
Async XLA Ops:
  6.5 309.8 %copy-start = (bf16[1,16,2048]{2,1,0:T(8,128)(2,1)S(1)}, bf16[1,16,2048]{2,1,0:T(8,128)(2,1)}, u32[]{:S(2)}) copy-start(bf16[1,16,2048]{2,1,0:T(8,128)(2,1)} %param.23) | copy-start | bytes 196612
  6.5 91.4 %all-gather.8.cloned.1.call-start = ((), (), s32[]{:S(2)}) async-start(), calls=%async_computation.4 | async-start | bytes 2129920 | tf_op jit(solution)/shard_map/all_gather | solution.py:50
  7.3 173.7 %all-gather.10.cloned.1.call-start = ((), (), s32[]{:S(2)}) async-start(), calls=%async_computation.5 | async-start | bytes 1064960 | tf_op jit(solution)/shard_map/all_gather | solution.py:51
  8.0 256.1 %all-gather.12.cloned.1.call-start = ((), (), s32[]{:S(2)}) async-start(), calls=%async_computation.6 | async-start | bytes 1064960 | tf_op jit(solution)/shard_map/all_gather | solution.py:50
  8.7 373.3 %reduce-scatter.3.cloned.1.call-start = ((), (), s32[]{:S(2)}) async-start(), calls=%async_computation.7 | async-start | bytes 884736 | tf_op jit(solution)/shard_map/reduce_scatter | solution.py:58
  100.4 80.6 %copy-start.1 = (bf16[192,2048]{1,0:T(8,128)(2,1)S(1)}, bf16[192,2048]{1,0:T(8,128)(2,1)}, u32[]{:S(2)}) copy-start(bf16[192,2048]{1,0:T(8,128)(2,1)} %param.14) | copy-start | bytes 2359300
  100.4 80.6 %copy-start.5 = (f32[2048]{0:T(1024)S(1)}, f32[2048]{0:T(1024)}, u32[]{:S(2)}) copy-start(f32[2048]{0:T(1024)} %param.17) | copy-start | bytes 24580
  182.9 85.0 %copy-start.3 = (s32[192,1]{0,1:T(1,128)S(1)}, s32[192,1]{0,1:T(1,128)}, u32[]{:S(2)}) copy-start(s32[192,1]{0,1:T(1,128)} %param.16) | copy-start | bytes 2308
  266.8 23.3 %copy-start.4 = (bf16[1,256,16]{1,2,0:T(8,128)(2,1)S(1)}, bf16[1,256,16]{1,2,0:T(8,128)(2,1)}, u32[]{:S(2)}) copy-start(bf16[1,256,16]{1,2,0:T(8,128)(2,1)} %param.22) | copy-start | bytes 24580
  266.8 142.6 %all-gather.14.cloned.1.call-start = ((), (), s32[]{:S(2)}) async-start(), calls=%async_computation.8 | async-start | bytes 3194880 | tf_op jit(solution)/shard_map/all_gather | solution.py:50
  267.4 214.2 %all-gather.16.cloned.1.call-start = ((), (), s32[]{:S(2)}) async-start(), calls=%async_computation.9 | async-start | bytes 3194880 | tf_op jit(solution)/shard_map/all_gather | solution.py:51
  270.1 19.9 %all-to-all-start = ((bf16[64,6,256]{2,1,0:T(8,128)(2,1)}), bf16[64,6,256]{2,1,0:T(8,128)(2,1)S(1)}, u32[]{:S(2)}, u32[]{:S(2)}) async-start(bf16[64,6,256]{2,1,0:T(8,128)(2,1)} %reshape.95), calls=%async_computation.1 | async-start | bytes 524288 | tf_op jit(solution)/shard_map/all_to_all | solution.py:117
  277.8 289.1 %all-gather.18.cloned.1.call-start = ((), (), s32[]{:S(2)}) async-start(), calls=%async_computation.10 | async-start | bytes 3194880 | tf_op jit(solution)/shard_map/all_gather | solution.py:51
  318.5 60.0 %all-to-all-start.1 = ((bf16[64,6,2048]{2,1,0:T(8,128)(2,1)}), bf16[64,6,2048]{2,1,0:T(8,128)(2,1)S(1)}, u32[]{:S(2)}, u32[]{:S(2)}) async-start(bf16[64,6,2048]{2,1,0:T(8,128)(2,1)} %reshape.97), calls=%async_computation.2 | async-start | bytes 4194304 | tf_op jit(solution)/shard_map/all_to_all | solution.py:131
  324.1 286.9 %reduce-scatter.5.cloned.1.call-start = ((), (), s32[]{:S(2)}) async-start(), calls=%async_computation.11 | async-start | bytes 884736 | tf_op jit(solution)/shard_map/reduce_scatter | solution.py:58
  382.0 27.4 %copy-start.6 = (f32[2048]{0:T(1024)S(1)}, f32[2048]{0:T(1024)}, u32[]{:S(2)}) copy-start(f32[2048]{0:T(1024)} %param.24) | copy-start | bytes 24580
  412.2 198.8 %copy-start.2 = (bf16[192,256]{1,0:T(8,128)(2,1)S(1)}, bf16[192,256]{1,0:T(8,128)(2,1)}, u32[]{:S(2)}) copy-start(bf16[192,256]{1,0:T(8,128)(2,1)} %reduce-scatter.3.cloned.1.call-done) | copy-start | bytes 294916
Sparse Core Ops, SparseCore 0:
  10.7 87.1 all-gather.7
  101.3 79.6 all-gather.9
  184.3 79.7 all-gather.11
  266.9 38.4 reduce-scatter.2
  309.1 87.0 all-gather.13
  399.9 81.5 all-gather.15
  485.4 81.3 all-gather.17
  572.7 38.2 reduce-scatter.4
